TPU v7x, 512 devices: a whole 4x4x16 slice. The times are simulated.
512 devices in a mesh: frame: 4 (over x), row: 16 (over z_hi, y), col: 8 (over z_lo, core).
Axes of the slice: x: 4, y: 4, z: 16 (z_hi: 4, z_lo: 4; z = z_hi * 4 + z_lo), core: 2. Of those that a mesh axis runs over, the one named last changes fastest.
Arguments:
- object_field: float32 [4096, 4096], P('row', 'col'), may hold values from -6 to 6
- images: float32 [4, 4096, 4096], P('frame', 'row', 'col'), may hold values from -6 to 6
- transfer_real: float32 [4, 4096, 4096], P('frame', ('row', 'col')), may hold values from -6 to 6
- transfer_imaginary: float32 [4, 4096, 4096], P('frame', ('row', 'col')), may hold values from -6 to 6
Outputs:
- gradient: float32 [4096, 4096], P(('frame', 'row'), 'col')
All inputs are finite; a program needn't handle non-finite values.
Results may differ from a plain program's by a relative error of at most 0.00011.
Values sent between devices are 32-bit elements; how exact they have to be, the bound alone decides.
A program may use at most 64 MiB of HBM per device.

v0:
```python
import math

import jax
import jax.numpy as jnp
from jax import lax
from jax.sharding import PartitionSpec as P


def fourier_block(length, sign_value):
    numbers = jnp.arange(length, dtype=jnp.int32)
    phases = numbers[:, None] * numbers[None, :] % length
    angles = sign_value * 2.0 * math.pi / length * phases.astype(jnp.float32)
    cosine = jnp.cos(angles)
    sine = jnp.sin(angles)
    return jnp.stack([jnp.stack([cosine, sine]), jnp.stack([-sine, cosine])])


def twiddle_table(outer_size, inner_size, sign_value):
    length = outer_size * inner_size
    outer_numbers = jnp.arange(outer_size, dtype=jnp.int32)
    inner_numbers = jnp.arange(inner_size, dtype=jnp.int32)
    phases = outer_numbers[:, None] * inner_numbers[None, :] % length
    angles = sign_value * 2.0 * math.pi / length * phases.astype(jnp.float32)
    return (jnp.cos(angles), jnp.sin(angles))


def transform(stacked, sign_value, want_imaginary, natural):
    highest = lax.Precision.HIGHEST
    length = stacked.shape[-1]
    inner_size = 128
    outer_size = length // inner_size
    leading = stacked.shape[:-1]
    plane_count = stacked.shape[0]
    shaped = stacked.reshape(leading + (outer_size, inner_size))
    opening = fourier_block(outer_size, sign_value)[:plane_count]
    middle = jnp.einsum("p...ab,pqak->q...kb", shaped, opening, precision=highest)
    twiddle_real, twiddle_imaginary = twiddle_table(outer_size, inner_size, sign_value)
    rotated = jnp.stack(
        [
            middle[0] * twiddle_real - middle[1] * twiddle_imaginary,
            middle[0] * twiddle_imaginary + middle[1] * twiddle_real,
        ]
    )
    output_count = 2 if want_imaginary else 1
    closing = fourier_block(inner_size, sign_value)[:, :output_count]
    result = jnp.einsum("p...kb,pqbm->q...km", rotated, closing, precision=highest)
    if natural:
        return jnp.swapaxes(result, -1, -2).reshape(result.shape[:-2] + (length,))
    return result


def deliver(packed, block_width):
    plane_count, frames, groups, piece_size = packed.shape
    local_rows = piece_size // block_width
    arrived = lax.all_to_all(packed, ("row", "col"), split_axis=2, concat_axis=2, tiled=True)
    unpacked = arrived.reshape(plane_count, frames, groups, local_rows, block_width).transpose(
        0, 1, 4, 2, 3
    )
    return unpacked.reshape(plane_count, frames, block_width, groups * local_rows)


def regroup_raw(spectra):
    plane_count, frames, local_rows, outer_size, inner_size = spectra.shape
    groups = lax.axis_size("row") * lax.axis_size("col")
    per_group = inner_size // groups
    packed = spectra.reshape(plane_count, frames, local_rows, outer_size, groups, per_group)
    packed = packed.transpose(0, 1, 4, 2, 5, 3).reshape(
        plane_count, frames, groups, local_rows * per_group * outer_size
    )
    return deliver(packed, per_group * outer_size)


def regroup_natural(planes_data):
    plane_count, frames, local_rows, length = planes_data.shape
    groups = lax.axis_size("row") * lax.axis_size("col")
    block_width = length // groups
    packed = planes_data.reshape(plane_count, frames, local_rows, groups, block_width)
    packed = packed.transpose(0, 1, 3, 2, 4).reshape(
        plane_count, frames, groups, local_rows * block_width
    )
    return deliver(packed, block_width)


def forward_plane(row_pencils):
    across = transform(row_pencils[None], -1.0, True, False)
    return transform(regroup_raw(across), -1.0, True, True)


def shards(object_field, images, transfer_real, transfer_imaginary):
    length = transfer_real.shape[2]
    inverse_scale = 1.0 / (float(length) * float(length))
    object_rows = lax.all_to_all(object_field[None], "col", split_axis=1, concat_axis=2, tiled=True)
    spectrum = forward_plane(object_rows)
    products = jnp.stack(
        [
            transfer_real * spectrum[0] - transfer_imaginary * spectrum[1],
            transfer_real * spectrum[1] + transfer_imaginary * spectrum[0],
        ]
    )
    across = transform(products, 1.0, True, False)
    modelled = transform(regroup_raw(across), 1.0, False, True)[0] * inverse_scale
    model_blocks = lax.all_to_all(modelled, "col", split_axis=2, concat_axis=1, tiled=True)
    weighted_blocks = (model_blocks - images) / (0.5 + jnp.abs(images))
    weighted = lax.all_to_all(weighted_blocks, "col", split_axis=1, concat_axis=2, tiled=True)
    residual_spectrum = forward_plane(weighted)
    adjoint_real = jnp.sum(
        transfer_real * residual_spectrum[0] + transfer_imaginary * residual_spectrum[1],
        axis=0,
        keepdims=True,
    )
    adjoint_imaginary = jnp.sum(
        transfer_real * residual_spectrum[1] - transfer_imaginary * residual_spectrum[0],
        axis=0,
        keepdims=True,
    )
    partial_inverse = transform(jnp.stack([adjoint_real, adjoint_imaginary]), 1.0, True, True)
    summed_all = lax.psum(partial_inverse, "frame")
    share_size = summed_all.shape[3] // lax.axis_size("frame")
    first_column = lax.axis_index("frame") * share_size
    shared = lax.dynamic_slice_in_dim(summed_all, first_column, share_size, 3)
    gradient_rows = transform(regroup_natural(shared), 1.0, False, True)[0] * inverse_scale
    gradient_blocks = lax.all_to_all(gradient_rows, "col", split_axis=2, concat_axis=1, tiled=True)
    return gradient_blocks[0]


def solution(mesh):
    placed = (
        P("row", "col"),
        P("frame", "row", "col"),
        P("frame", ("row", "col"), None),
        P("frame", ("row", "col"), None),
    )
    return jax.shard_map(
        shards, mesh=mesh, in_specs=placed, out_specs=P(("frame", "row"), "col"), check_vma=False
    )
```

profile of v0, /device:TPU:1, one launch (start us, length us, event | category | flops | bytes accessed | tf_op | source)
XLA Modules:
  0.0 498.2 jit_solution(9323601812973492109)
XLA Ops:
  6.5 2.2 broadcast_in_dim.2
  8.7 10.3 %all-to-all-start = ((f32[1,256,512]{2,0,1:T(1,128)}), f32[1,256,512]{2,0,1:T(1,128)S(1)}, u32[]{:S(2)}, u32[]{:S(2)}) async-start(f32[1,256,512]{2,0,1:T(1,128)} %broadcast_in_dim.2), calls=%async_computation | async-start | bytes 1048576 | tf_op jit(solution)/shard_map/all_to_all | solution.py:92
  19.8 13.7 %all-to-all-done = f32[1,256,512]{2,0,1:T(1,128)S(1)} async-done(((f32[1,256,512]{2,0,1:T(1,128)}), f32[1,256,512]{2,0,1:T(1,128)S(1)}, u32[]{:S(2)}, u32[]{:S(2)}) %all-to-all-start) | async-done | bytes 524320 | tf_op jit(solution)/shard_map/all_to_all | solution.py:92
  35.0 1.0 fusion.17
  36.0 1.3 copy.100
  37.3 14.6 %all-to-all-start.1 = ((f32[2,1,128,1024]{3,0,1,2:T(2,128)}), f32[2,1,128,1024]{3,0,1,2:T(2,128)S(1)}, u32[]{:S(2)}, u32[]{:S(2)}) async-start(f32[2,1,128,1024]{3,0,1,2:T(2,128)} %copy.100), calls=%async_computation.1 | async-start | bytes 2097152 | tf_op jit(solution)/shard_map/all_to_all | solution.py:55
  53.2 54.4 %all-to-all-done.1 = f32[2,1,128,1024]{3,0,1,2:T(2,128)S(1)} async-done(((f32[2,1,128,1024]{3,0,1,2:T(2,128)}), f32[2,1,128,1024]{3,0,1,2:T(2,128)S(1)}, u32[]{:S(2)}, u32[]{:S(2)}) %all-to-all-start.1) | async-done | bytes 1048608 | tf_op jit(solution)/shard_map/all_to_all | solution.py:55
  108.1 2.7 copy.187
  110.8 3.3 reshape.615
  114.1 1.1 convolution_bitcast_fusion.9
  115.3 1.0 convolution_bitcast_fusion.8
  118.8 1.6 copy.107
  120.4 1.8 squeeze.11
  122.2 1.5 subtract_bitcast_fusion.1
  123.9 1.1 convolution_bitcast_fusion.7
  125.2 1.0 fusion.14
  126.8 62.4 %all_to_all.83 = f32[2,1,128,1024]{3,0,1,2:T(2,128)S(1)} all-to-all(f32[2,1,128,1024]{3,0,1,2:T(2,128)S(1)} %copy.111), channel_id=1, replica_groups=mesh['frame'=4,'row'=16,'col'=8] {'row','col'}, dimensions={2} | all-to-all | bytes 2097152 | tf_op jit(solution)/shard_map/all_to_all | solution.py:55
  189.7 2.7 copy.188
  192.4 3.3 reshape.626
  195.7 1.1 convolution_bitcast_fusion.6
  197.0 1.0 fusion.1
  198.0 1.9 copy.189
  200.4 19.3 %reduce = f32[4096,32]{1,0:T(8,128)} reduce(f32[4096,1,32]{2,1,0:T(1,128)S(1)} %bitcast.348, f32[]{:T(128)} %broadcast.724), dimensions={1}, to_apply=%bitcast.307.reduce_sub_computation | reduce | bytes 1048580
  219.7 2.5 reshape.658
  222.2 19.1 %all_to_all.84 = f32[8,1,16384]{2,1,0:T(1,128)S(1)} all-to-all(f32[8,1,16384]{2,1,0:T(1,128)S(1)} %reshape.658), channel_id=1, replica_groups=mesh['frame'=4,'row'=16,'col'=8] {'col'}, dimensions={0} | all-to-all | bytes 1048576 | tf_op jit(solution)/shard_map/all_to_all | solution.py:102
  241.3 1.8 reduce.1
  243.1 3.5 reshape.659
  247.6 1.1 fusion.25
  249.3 17.8 %all_to_all.85 = f32[1,256,512]{2,0,1:T(1,128)S(1)} all-to-all(f32[1,256,512]{2,0,1:T(1,128)S(1)} %copy.121), channel_id=1, replica_groups=mesh['frame'=4,'row'=16,'col'=8] {'col'}, dimensions={1} | all-to-all | bytes 1048576 | tf_op jit(solution)/shard_map/all_to_all | solution.py:104
  268.6 1.0 fusion.12
  270.2 62.6 %all_to_all.86 = f32[2,1,128,1024]{3,0,1,2:T(2,128)S(1)} all-to-all(f32[2,1,128,1024]{3,0,1,2:T(2,128)S(1)} %copy.124), channel_id=1, replica_groups=mesh['frame'=4,'row'=16,'col'=8] {'row','col'}, dimensions={2} | all-to-all | bytes 2097152 | tf_op jit(solution)/shard_map/all_to_all | solution.py:55
  333.4 2.7 copy.191
  336.0 3.3 reshape.634
  339.4 1.1 convolution_bitcast_fusion.5
  340.6 1.0 convolution_bitcast_fusion.4
  344.8 1.3 add_bitcast_fusion
  346.4 1.1 convolution_bitcast_fusion.3
  347.7 1.0 convolution_bitcast_fusion.2
  348.7 2.7 copy.135
  351.4 4.3 reshape.603
  355.8 51.6 %all-reduce.2.cloned.1.call-done = f32[2,1,32,4096]{3,2,0,1:T(8,128)} async-done(((f32[2,1,32,4096]{3,2,0,1:T(8,128)}), f32[2,1,32,4096]{3,2,0,1:T(8,128)}) %all-reduce.2.cloned.1.call-update) | async-done | bytes 1048592 | tf_op jit(solution)/shard_map/psum | solution.py:117
  409.2 41.7 %all_to_all.87 = f32[2,1,128,256]{3,0,1,2:T(2,128)S(1)} all-to-all(f32[2,1,128,256]{3,0,1,2:T(2,128)S(1)} %copy.138), channel_id=1, replica_groups=mesh['frame'=4,'row'=16,'col'=8] {'row','col'}, dimensions={2} | all-to-all | bytes 524288 | tf_op jit(solution)/shard_map/all_to_all | solution.py:55
  452.6 1.9 copy.193
  454.4 19.3 %reduce.2 = f32[4096,8]{1,0:T(8,128)} reduce(f32[4096,1,8]{2,1,0:T(1,128)S(1)} %bitcast.349, f32[]{:T(128)} %broadcast.724), dimensions={1}, to_apply=%bitcast.309.reduce_sub_computation | reduce | bytes 262148
  473.7 2.7 reshape.660
  476.4 8.8 %all_to_all.88 = f32[8,1,4096]{2,1,0:T(1,128)S(1)} all-to-all(f32[8,1,4096]{2,1,0:T(1,128)S(1)} %reshape.660), channel_id=1, replica_groups=mesh['frame'=4,'row'=16,'col'=8] {'col'}, dimensions={0} | all-to-all | bytes 262144 | tf_op jit(solution)/shard_map/all_to_all | solution.py:122
  486.1 3.5 reshape.661
  489.6 1.2 copy.146
  (113 shorter events, 20.8 us)
Async XLA Ops:
  8.7 24.8 %all-to-all-start = ((f32[1,256,512]{2,0,1:T(1,128)}), f32[1,256,512]{2,0,1:T(1,128)S(1)}, u32[]{:S(2)}, u32[]{:S(2)}) async-start(f32[1,256,512]{2,0,1:T(1,128)} %broadcast_in_dim.2), calls=%async_computation | async-start | bytes 1048576 | tf_op jit(solution)/shard_map/all_to_all | solution.py:92
  19.1 33.7 %copy-start.22 = (f32[1,32,32]{1,2,0:T(8,128)}, f32[1,32,32]{1,2,0:T(8,128)S(1)}, u32[]{:S(2)}) copy-start(f32[1,32,32]{1,2,0:T(8,128)S(1)} %get-tuple-element.37) | copy-start | bytes 12292
  19.1 33.7 %copy-start.24 = (f32[1,32,32]{1,2,0:T(8,128)}, f32[1,32,32]{1,2,0:T(8,128)S(1)}, u32[]{:S(2)}) copy-start(f32[1,32,32]{1,2,0:T(8,128)S(1)} %get-tuple-element.38) | copy-start | bytes 12292
  19.2 96.0 %copy-start.9 = (f32[32,128]{1,0:T(8,128)}, f32[32,128]{1,0:T(8,128)S(1)}, u32[]{:S(2)}) copy-start(f32[32,128]{1,0:T(8,128)S(1)} %get-tuple-element.40) | copy-start | bytes 49156
  37.3 70.3 %all-to-all-start.1 = ((f32[2,1,128,1024]{3,0,1,2:T(2,128)}), f32[2,1,128,1024]{3,0,1,2:T(2,128)S(1)}, u32[]{:S(2)}, u32[]{:S(2)}) async-start(f32[2,1,128,1024]{3,0,1,2:T(2,128)} %copy.100), calls=%async_computation.1 | async-start | bytes 2097152 | tf_op jit(solution)/shard_map/all_to_all | solution.py:55
  51.9 355.5 %all-reduce.2.cloned.1.call-start = ((), (), s32[]{:S(2)}) async-start(), calls=%async_computation.8 | async-start | bytes 2097152 | tf_op jit(solution)/shard_map/psum | solution.py:117
  52.5 72.4 %copy-start.12 = (f32[32,128]{1,0:T(8,128)}, f32[32,128]{1,0:T(8,128)S(1)}, u32[]{:S(2)}) copy-start(f32[32,128]{1,0:T(8,128)S(1)} %get-tuple-element.45) | copy-start | bytes 49156
  52.5 72.4 %copy-start.15 = (f32[32,128]{1,0:T(8,128)}, f32[32,128]{1,0:T(8,128)S(1)}, u32[]{:S(2)}) copy-start(f32[32,128]{1,0:T(8,128)S(1)} %get-tuple-element.46) | copy-start | bytes 49156
  52.8 61.2 %copy-start.18 = (f32[1,2,32,32]{2,3,1,0:T(8,128)}, f32[1,2,32,32]{2,3,1,0:T(8,128)S(1)}, u32[]{:S(2)}) copy-start(f32[1,2,32,32]{2,3,1,0:T(8,128)S(1)} %get-tuple-element.35) | copy-start | bytes 24580
  52.9 61.2 %copy-start.20 = (f32[1,2,32,32]{2,3,1,0:T(8,128)}, f32[1,2,32,32]{2,3,1,0:T(8,128)S(1)}, u32[]{:S(2)}) copy-start(f32[1,2,32,32]{2,3,1,0:T(8,128)S(1)} %get-tuple-element.36) | copy-start | bytes 24580
  52.9 71.0 %copy-start.3 = (f32[1,2,32,32]{2,3,1,0:T(8,128)}, f32[1,2,32,32]{2,3,1,0:T(8,128)S(1)}, u32[]{:S(2)}) copy-start(f32[1,2,32,32]{2,3,1,0:T(8,128)S(1)} %get-tuple-element.33) | copy-start | bytes 24580
  52.9 71.0 %copy-start.6 = (f32[1,2,32,32]{2,3,1,0:T(8,128)}, f32[1,2,32,32]{2,3,1,0:T(8,128)S(1)}, u32[]{:S(2)}) copy-start(f32[1,2,32,32]{2,3,1,0:T(8,128)S(1)} %get-tuple-element.34) | copy-start | bytes 24580
  53.2 71.9 %copy-start = (f32[1,2,128,128]{3,2,1,0:T(8,128)}, f32[1,2,128,128]{3,2,1,0:T(8,128)S(1)}, u32[]{:S(2)}) copy-start(f32[1,2,128,128]{3,2,1,0:T(8,128)S(1)} %get-tuple-element.30) | copy-start | bytes 393220
  192.4 3.3 copy-start.4
  192.4 3.3 copy-start.7
  195.7 1.1 copy-start.13
  195.7 1.1 copy-start.16
  195.7 1.3 copy-start.1
  248.7 18.7 %copy-start.23 = (f32[1,32,32]{1,2,0:T(8,128)S(1)}, f32[1,32,32]{1,2,0:T(8,128)}, u32[]{:S(2)}) copy-start(f32[1,32,32]{1,2,0:T(8,128)} %copy-done.22) | copy-start | bytes 12292
  248.7 18.7 %copy-start.25 = (f32[1,32,32]{1,2,0:T(8,128)S(1)}, f32[1,32,32]{1,2,0:T(8,128)}, u32[]{:S(2)}) copy-start(f32[1,32,32]{1,2,0:T(8,128)} %copy-done.24) | copy-start | bytes 12292
  267.1 1.4 copy-start.10
  336.0 3.3 copy-start.19
  336.0 3.3 copy-start.21
  339.4 1.1 copy-start.11
  344.8 1.6 copy-start.5
  344.8 1.6 copy-start.8
  346.2 1.3 copy-start.14
  346.2 1.3 copy-start.17
  346.4 1.3 copy-start.2
Sparse Core Ops, SparseCore 0:
  355.9 51.4 all-reduce.1
where the time goes:
time: 504 us; the launch traced here: 498 us
  blocking collectives  212 us (42%)
  waiting for transfers between devices  120 us (24%)
  local copies, waits for them, and re-layouts  63.1 us (13%)
  other arithmetic  48 us (10%)
  starting transfers between devices  25.1 us (5%)
  matrix products  15 us (3%)
  between operations  14.8 us (3%)
    all_to_all x3, blocking collectives, deliver(): lax.all_to_all(packed, ('row', 'col'), split_axis=2, concat_axis=2, tiled...  167 us
    all_to_all x1, waiting for transfers between devices, deliver(): lax.all_to_all(packed, ('row', 'col'), split_axis=2, concat_axis=2, tiled...  54.4 us
    psum x1, waiting for transfers between devices, shards(): summed_all = lax.psum(partial_inverse, 'frame')  51.6 us
    unnamed x4, other arithmetic  41.4 us
    all_to_all x1, blocking collectives, shards(): lax.all_to_all(modelled, 'col', split_axis=2, concat_axis=1, tiled=True)  19.1 us
    another operation x10, local copies, waits for them, and re-layouts  18.6 us
    all_to_all x1, blocking collectives, shards(): lax.all_to_all(weighted_blocks, 'col', split_axis=1, concat_axis=2, tiled...  17.8 us
    all_to_all x1, starting transfers between devices, deliver(): lax.all_to_all(packed, ('row', 'col'), split_axis=2, concat_axis=2, tiled...  14.6 us
  transfers between devices with their start and end apart: 3, of which 3 were waited for; matrix products, arithmetic and copies ran while one was open for 0% of the time, Pallas kernels for 0%

commit v1 on v0

v1 whole, which is shorter than its diff:
```python
import functools
import math

import jax
import jax.numpy as jnp
import ml_dtypes
import numpy as np
from jax import lax
from jax.experimental import pallas as pl
from jax.experimental.pallas import tpu as pltpu
from jax.sharding import PartitionSpec as P

F32 = jnp.float32
BF16 = jnp.bfloat16
MESH = pl.DeviceIdType.MESH

N = 4096
DEVICES = 128


def block_of(g):
    return np.where(g < 64, 2 * g, 2 * (127 - g) + 1)


def halves(table):
    high = table.astype(np.float32).astype(ml_dtypes.bfloat16)
    low = (table - high.astype(np.float64)).astype(np.float32).astype(ml_dtypes.bfloat16)
    return high, low


def turn(numbers, length):
    angles = 2.0 * math.pi / length * (numbers % length)
    return np.cos(angles), np.sin(angles)


def vertical_forward(order):
    cosine, sine = turn(np.arange(512)[:, None] * order[None, :], 512)
    pieces = []
    for chunk in range(4):
        rows = slice(128 * chunk, 128 * chunk + 128)
        high, low = halves(np.concatenate([cosine[rows], -sine[rows]], 0))
        pieces += [high, low]
    return np.concatenate(pieces, 0)


def vertical_inverse(order):
    cosine, sine = turn(order[:, None] * np.arange(512)[None, :], 512)
    whole = np.concatenate([sine, cosine, -sine], 1)
    pieces = []
    for chunk in range(4):
        pieces += list(halves(whole[128 * chunk : 128 * chunk + 128]))
    return np.concatenate(pieces, 0)


def tables():
    made = {}
    g = np.arange(128)
    full = (4 * g[None, :] + np.arange(4)[:, None]).reshape(-1)
    f, r, c = np.meshgrid(np.arange(4), np.arange(16), np.arange(8), indexing="ij")
    made["down_object"] = vertical_forward((32 * r + 8 * f + c).reshape(-1))
    made["down_full"] = vertical_forward(full)
    made["up_full"] = vertical_inverse(full)
    f, c, r = np.meshgrid(np.arange(4), np.arange(8), np.arange(16), indexing="ij")
    made["up_gradient"] = vertical_inverse((128 * f + 8 * r + c).reshape(-1))

    s, t = np.meshgrid(np.arange(16), np.arange(8), indexing="ij")
    s, t = s.reshape(-1), t.reshape(-1)
    sh, v1, sl = np.meshgrid(np.arange(2), np.arange(8), np.arange(8), indexing="ij")
    spectral_s, spectral_v = (8 * sh + sl).reshape(-1), v1.reshape(-1)
    cosine, sine = turn(t[:, None] * spectral_v[None, :], 8)
    same = (s[:, None] == spectral_s[None, :]).astype(np.float64)
    cosine, sine = cosine * same, sine * same
    made["mix_down"] = np.concatenate(halves(np.block([[cosine, -sine], [sine, cosine]])), 0)
    made["mix_up"] = np.concatenate(halves(np.block([[cosine.T, sine.T], [-sine.T, cosine.T]])), 0)
    cosine, sine = turn(np.arange(512)[:, None] * t[None, :], 4096)
    made["twist_vertical"] = np.concatenate([cosine, sine], 0).astype(np.float32)

    x1, tx = s, t
    same = (t[:, None] == tx[None, :]).astype(np.float64)
    cosine, sine = turn(s[:, None] * x1[None, :], 16)
    cosine, sine = cosine * same, sine * same
    made["open_x"] = np.concatenate(halves(np.concatenate([cosine, -sine], 0)), 0)
    scale = 1.0 / (float(N) * float(N))
    made["close_x"] = np.concatenate(halves(np.concatenate([cosine.T, -sine.T], 1) * scale), 0)
    cosine, sine = turn(s[:, None] * np.arange(256)[None, :], 4096)
    made["twist_out"] = np.concatenate([cosine, sine], 0).astype(np.float32)
    made["twist_in"] = np.concatenate([cosine.T, sine.T], 0).astype(np.float32)

    def across(order):
        cosine, sine = turn(block_of(order)[:, None] * np.arange(256)[None, :], 256)
        alternate = np.zeros((16, 512))
        alternate[0, :256] = 1.0 - 2.0 * (np.arange(256) % 2)
        whole = np.concatenate(
            [np.concatenate([cosine, sine], 1), np.concatenate([-sine, cosine], 1), alternate], 0
        )
        return np.concatenate(halves(whole), 0)

    made["across_full"] = across(g)
    c, r = np.meshgrid(np.arange(8), np.arange(16), indexing="ij")
    made["across_object"] = across((8 * r + c).reshape(-1))
    cosine, sine = turn(np.arange(256)[:, None] * block_of(g)[None, :], 256)
    made["back_x"] = np.concatenate(halves(np.block([[cosine, -sine], [sine, cosine]])), 0)

    choose = np.zeros((3, 384, 512))
    for kind in range(3):
        for row in range(128):
            slot, v = spectral_s[row], spectral_v[row]

            def own(number):
                return (number // 8) * 64 + v * 8 + number % 8

            def got(number):
                return 256 + (number // 8) * 64 + v * 8 + number % 8

            extra = 384 + v
            if kind == 2:
                plus, minus = got(slot), own(16 - slot)
            else:
                plus, minus = own(slot), (extra if slot == 0 else got(16 - slot))
            if kind == 0 and slot == 0:
                choose[kind, row, plus] = 1.0
                choose[kind, 128 + row, minus] = 1.0
            else:
                for part, sign in ((0, 1.0), (128, 1.0), (256, -1.0)):
                    choose[kind, part + row, plus] = 1.0
                    choose[kind, part + row, minus] = sign
    made["choose"] = choose.astype(ml_dtypes.bfloat16)
    return made


def product(left, right):
    return lax.dot_general(left, right, (((1,), (0,)), ((), ())), preferred_element_type=F32)


def product_turned(left, right):
    return lax.dot_general(left, right, (((1,), (1,)), ((), ())), preferred_element_type=F32)


def split(values):
    high = values.astype(BF16)
    return high, (values - high.astype(F32)).astype(BF16)


def table_first(table, high, low, dot):
    rows = table.shape[0] // 2
    both = dot(table, high)
    return both[:rows] + (both[rows:] + dot(table[:rows], low))


def table_last(values, table):
    depth = table.shape[0] // 2
    rows = values.shape[0]
    high, low = split(values)
    both = product(jnp.concatenate([high, low], 0), table[:depth])
    return both[:rows] + (both[rows:] + product(high, table[depth:]))


def rows_to_half(field, tab, across):
    opened = table_first(tab["open_x"][...], *split(field), product)
    real, imaginary = opened[:128], opened[128:]
    cosine, sine = tab["twist_out"][:128, :], tab["twist_out"][128:, :]
    turned = jnp.concatenate(
        [real * cosine + imaginary * sine, imaginary * cosine - real * sine], 1
    )
    out = table_first(tab[across][...], *split(turned), product_turned)
    row = lax.broadcasted_iota(jnp.int32, (128, 128), 0)
    lane = lax.broadcasted_iota(jnp.int32, (128, 128), 1)
    extra = jnp.where((row == 0) & (lane < 8), out[256:257], 0.0)
    return out[:128], out[128:256] + extra


def half_to_rows(planes, tab):
    back = table_first(tab["back_x"][...], *split(planes), product)
    lane = lax.broadcasted_iota(jnp.int32, (256, 128), 1)
    number = lax.broadcasted_iota(jnp.int32, (256, 128), 0)
    shared = jnp.where(lane < 8, planes[128:129], 0.0)
    real = back[:256] + jnp.where(number % 2 == 0, shared, -shared)
    imaginary = back[256:]
    cosine, sine = tab["twist_in"][:256, :], tab["twist_in"][256:, :]
    turned = jnp.concatenate(
        [real * cosine - imaginary * sine, real * sine + imaginary * cosine], 1
    )
    return table_first(tab["close_x"][...], *split(turned), product_turned)


def spectral_chunk(table, high, low, cosine, sine, tab, weights, conjugate):
    opened = table_first(table, high, low, product)
    real, imaginary = opened[:128], opened[128:]
    cosine2 = jnp.concatenate([cosine, cosine], 1)
    sine2 = jnp.concatenate([sine, sine], 1)
    turned_real = real * cosine2 + imaginary * sine2
    turned_imaginary = imaginary * cosine2 - real * sine2
    stacked = jnp.concatenate(
        [
            jnp.concatenate([turned_real[:, :128], turned_imaginary[:, :128]], 1),
            jnp.concatenate([turned_real[:, 128:], turned_imaginary[:, 128:]], 1),
        ],
        0,
    )
    mixed = table_last(stacked, tab["mix_down"][...])
    ar, ai = mixed[:128, :128], mixed[:128, 128:]
    br, bi = mixed[128:, :128], mixed[128:, 128:]
    (s1r, s1i), (s2r, s2i), (dr, di) = weights
    if conjugate:
        s1i, s2i, di = -s1i, -s2i, -di
    ur = s1r * ar - s1i * ai - (dr * bi + di * br)
    ui = s1r * ai + s1i * ar + (dr * br - di * bi)
    vr = dr * ar - di * ai - (s2r * bi + s2i * br)
    vi = dr * ai + di * ar + (s2r * br - s2i * bi)
    stacked = jnp.concatenate(
        [jnp.concatenate([ur, ui], 1), jnp.concatenate([vr, vi], 1)], 0
    )
    mixed = table_last(stacked, tab["mix_up"][...])
    cosine = jnp.concatenate([cosine, cosine], 0)
    sine = jnp.concatenate([sine, sine], 0)
    real, imaginary = mixed[:, :128], mixed[:, 128:]
    return real * cosine - imaginary * sine, real * sine + imaginary * cosine


NAMES = (
    "open_x",
    "twist_out",
    "across_object",
    "down_object",
    "twist_vertical",
    "mix_down",
    "choose",
    "mix_up",
    "up_full",
    "back_x",
    "twist_in",
    "close_x",
    "across_full",
    "down_full",
    "up_gradient",
)


def kernel(*refs):
    object_ref, images_ref, real_ref, imaginary_ref = refs[:4]
    sources = refs[4 : 4 + len(NAMES)]
    out_ref = refs[4 + len(NAMES)]
    rest = refs[5 + len(NAMES) :]
    tab = dict(zip(NAMES, rest[: len(NAMES)]))
    (
        transfer,
        partner,
        extra_send,
        extra,
        object_rows,
        image_rows,
        send_a,
        got_a,
        send_b,
        pencils,
        weight,
        split_high,
        split_low,
        back_high,
        back_low,
        send_four,
        got_four,
        send_five,
        got_five,
        send_six,
        got_six,
        send_c,
        got_c,
        send_d,
        got_d,
        send_out,
        got_out,
        table_sem,
        local_sem,
        send_sem,
        recv_sem,
    ) = rest[len(NAMES) :]

    frame, row, col = lax.axis_index("frame"), lax.axis_index("row"), lax.axis_index("col")
    me = row * 8 + col

    loads = {
        name: pltpu.make_async_copy(source, tab[name], table_sem.at[number])
        for number, (name, source) in enumerate(zip(NAMES, sources))
    }

    def need(*names):
        for name in names:
            loads[name].wait()

    transfer_loads = [
        pltpu.make_async_copy(real_ref, transfer.at[0], local_sem.at[0]),
        pltpu.make_async_copy(imaginary_ref, transfer.at[1], local_sem.at[1]),
    ]
    object_load = pltpu.make_async_copy(
        object_ref.at[8 * frame + col], object_rows.at[col], local_sem.at[2]
    )
    images_load = pltpu.make_async_copy(
        images_ref.at[pl.ds(4 * col, 4)], image_rows.at[col], local_sem.at[3]
    )
    for load in transfer_loads:
        load.start()
    object_load.start()
    images_load.start()
    for name in NAMES:
        loads[name].start()

    barrier = pltpu.get_barrier_semaphore()

    def greet(step, carry):
        other = lax.rem(me + step, DEVICES)
        pl.semaphore_signal(
            barrier, inc=1, device_id=(frame, other // 8, lax.rem(other, 8)), device_id_type=MESH
        )
        return carry

    lax.fori_loop(1, DEVICES, greet, 0)
    for step in range(1, 4):
        pl.semaphore_signal(
            barrier, inc=1, device_id=(lax.rem(frame + step, 4), row, col), device_id_type=MESH
        )
    pl.semaphore_wait(barrier, DEVICES - 1 + 3)

    def send(source, target, phase, device):
        pltpu.make_async_remote_copy(
            src_ref=source,
            dst_ref=target,
            send_sem=send_sem.at[phase],
            recv_sem=recv_sem.at[phase],
            device_id=device,
            device_id_type=MESH,
        ).start()

    def wait_bytes(like, semaphore):
        pltpu.make_async_copy(like, like, semaphore).wait()

    def each_col(body):
        def step(number, carry):
            body(lax.rem(col + number, 8))
            return carry

        lax.fori_loop(1, 8, step, 0)

    def each_row(body):
        def step(number, carry):
            body(lax.rem(row + number, 16))
            return carry

        lax.fori_loop(1, 16, step, 0)

    def each_frame(body):
        for number in range(1, 4):
            body(lax.rem(frame + number, 4))

    def tile(number):
        return pl.ds(pl.multiple_of(number * 8, 8), 8)

    each_col(
        lambda c: send(
            object_ref.at[8 * frame + c], object_rows.at[col], 0, (frame, row, c)
        )
    )
    for load in transfer_loads:
        load.wait()
    for plane in range(2):
        extra_send[plane] = transfer[plane, 0, pl.ds(0, 32, stride=8), :]
    opposite = 127 - me
    is_end = 1 - (lax.rem(me, 64) + 63) // 64
    beyond = 128 - me - 64 * is_end
    send(extra_send, extra, 2, (frame, beyond // 8, lax.rem(beyond, 8)))
    for plane in range(2):
        send(
            transfer.at[plane, pl.ds(2, 2)],
            partner.at[plane],
            3 + plane,
            (frame, opposite // 8, lax.rem(opposite, 8)),
        )
    each_col(
        lambda c: send(
            images_ref.at[pl.ds(4 * c, 4)], image_rows.at[col], 1, (frame, row, c)
        )
    )

    def field_of(read):
        return jnp.concatenate(
            [
                jnp.concatenate([read(x1 // 2, 2 * (x1 % 2) + part) for x1 in range(16)], 0)
                for part in range(2)
            ],
            1,
        )

    object_load.wait()
    wait_bytes(object_rows.at[pl.ds(0, 7)], recv_sem.at[0])
    need("open_x", "twist_out", "across_object")
    planes = rows_to_half(field_of(lambda c, k: object_rows[c, k]), tab, "across_object")
    for plane in range(2):
        for c in range(8):
            send_a[c, plane] = planes[plane][16 * c : 16 * c + 16]
    got_a[pl.ds(pl.multiple_of(col * 32, 32), 32), :] = send_a[col].reshape(32, 128)
    each_col(
        lambda c: send(
            send_a.at[c].reshape(32, 128),
            got_a.at[pl.ds(pl.multiple_of(col * 32, 32), 32)],
            5,
            (frame, row, c),
        )
    )

    def cross_rows(got, sends, phase, target):
        wait_bytes(got.at[pl.ds(0, 7 * 32)], recv_sem.at[phase])
        for r in range(16):
            sends[r] = got[pl.ds(r, 16, stride=16), :]
        target[row] = sends[row]
        each_row(lambda r: send(sends.at[r], target.at[row], phase + 1, (frame, r, col)))
        wait_bytes(sends.at[pl.ds(0, 15)], recv_sem.at[phase + 1])

    def quarter(number):
        return pencils.at[pl.ds(pl.multiple_of(number * 16, 16), 16)]

    cross_rows(got_a, send_b, 5, quarter(frame))
    each_frame(lambda f: send(quarter(frame), quarter(frame), 7, (f, row, col)))
    wait_bytes(pencils.at[pl.ds(0, 48)], recv_sem.at[7])

    wait_bytes(extra, recv_sem.at[2])
    for plane in range(2):
        wait_bytes(partner.at[plane], recv_sem.at[3 + plane])
    need("choose")
    kind = (me + 127) // 128 + me // 64
    for part in range(4):
        blocks = []
        for plane in range(2):
            rows = [
                transfer[plane, a, pl.ds((4 * v + part) * 8, 8), :]
                for a in range(4)
                for v in range(8)
            ]
            rows += [
                partner[plane, a, pl.ds((4 * v + part) * 8, 8), :]
                for a in range(2)
                for v in range(8)
            ]
            rows += [extra[plane, pl.ds(part, 8, stride=4), :], jnp.zeros((120, 128), F32)]
            blocks.append(jnp.concatenate(rows, 0))
        block = jnp.concatenate(blocks, 1)
        first = block.astype(BF16)
        left = block - first.astype(F32)
        second = left.astype(BF16)
        third = (left - second.astype(F32)).astype(BF16)
        chosen = tab["choose"][kind]
        picked = product(chosen, first) + (product(chosen, second) + product(chosen, third))
        for number in range(3):
            for plane in range(2):
                weight[number, plane, pl.ds(128 * part, 128), :] = picked[
                    128 * number : 128 * number + 128, 128 * plane : 128 * plane + 128
                ].T

    def through(down, conjugate):
        def chunk(number, carry):
            rows = pl.ds(pl.multiple_of(number * 128, 128), 128)
            weights = [(weight[k, 0, rows, :], weight[k, 1, rows, :]) for k in range(3)]
            real, imaginary = spectral_chunk(
                tab[down][pl.ds(pl.multiple_of(number * 512, 512), 512), :],
                split_high[...],
                split_low[...],
                tab["twist_vertical"][rows, :],
                tab["twist_vertical"][pl.ds(pl.multiple_of(512 + number * 128, 128), 128), :],
                tab,
                weights,
                conjugate,
            )
            for plane, values in enumerate((real, imaginary)):
                high, low = split(values)
                for which in range(2):
                    part = slice(128 * which, 128 * which + 128)
                    at = pl.ds(pl.multiple_of(512 * plane + number * 128, 128), 128)
                    back_high[which, at, :] = high[part]
                    back_low[which, at, :] = low[part]
            return carry

        lax.fori_loop(0, 4, chunk, 0)

    def return_chunk(up, number):
        table = tab[up][pl.ds(pl.multiple_of(number * 256, 256), 256), :]
        real = table_first(table[:, 512:], back_high[0], back_low[0], product)
        imaginary = table_first(table[:, :1024], back_high[1], back_low[1], product)
        return real, imaginary

    def to_all(source, target, phase):
        target[tile(me), :] = source[tile(me), :]

        def step(number, carry):
            other = lax.rem(me + number, DEVICES)
            send(
                source.at[tile(other)],
                target.at[tile(me)],
                phase,
                (frame, other // 8, lax.rem(other, 8)),
            )
            return carry

        lax.fori_loop(1, DEVICES, step, 0)

    for plane in range(2):
        high, low = split(
            pencils.reshape(1024, 128)[pl.ds(plane, 512, stride=2), :]
        )
        split_high[:, 128 * plane : 128 * plane + 128] = high
        split_low[:, 128 * plane : 128 * plane + 128] = low
    need("down_object", "twist_vertical", "mix_down", "mix_up")
    through("down_object", False)
    need("up_full")
    for number in range(4):
        real, imaginary = return_chunk("up_full", number)
        send_four[pl.ds(number, 128, stride=8), :] = real
        send_four[pl.ds(4 + number, 128, stride=8), :] = imaginary
    to_all(send_four, got_four, 8)

    images_load.wait()
    wait_bytes(image_rows.at[pl.ds(0, 7)], recv_sem.at[1])
    need("back_x", "twist_in", "close_x", "across_full")
    wait_bytes(got_four.at[pl.ds(0, 127 * 8)], recv_sem.at[8])
    for number in range(4):
        modelled = half_to_rows(
            jnp.concatenate(
                [
                    got_four[pl.ds(number, 128, stride=8), :],
                    got_four[pl.ds(4 + number, 128, stride=8), :],
                ],
                0,
            ),
            tab,
        )
        images = field_of(lambda c, k: image_rows[c, number, k])
        weighted = (modelled - images) / (0.5 + jnp.abs(images))
        planes = rows_to_half(weighted, tab, "across_full")
        for plane in range(2):
            send_five[pl.ds(4 * plane + number, 128, stride=8), :] = planes[plane]
    to_all(send_five, got_five, 9)

    need("down_full", "up_gradient")
    wait_bytes(got_five.at[pl.ds(0, 127 * 8)], recv_sem.at[9])
    for plane in range(2):
        for number in range(4):
            high, low = split(got_five[pl.ds(4 * plane + number, 128, stride=8), :])
            at = (slice(128 * number, 128 * number + 128), slice(128 * plane, 128 * plane + 128))
            split_high[at] = high
            split_low[at] = low
    through("down_full", True)
    for number in range(4):
        planes = return_chunk("up_gradient", number)
        for plane in range(2):
            for c in range(8):
                send_six[number, c, plane] = planes[plane][16 * c : 16 * c + 16]

    each_frame(lambda f: send(send_six.at[f], got_six.at[frame], 10, (f, row, col)))
    got_six[frame] = send_six[frame]
    wait_bytes(send_six.at[pl.ds(0, 3)], recv_sem.at[10])
    send_c[...] = (got_six[0] + got_six[1]) + (got_six[2] + got_six[3])
    got_c[pl.ds(pl.multiple_of(col * 32, 32), 32), :] = send_c[col].reshape(32, 128)
    each_col(
        lambda c: send(
            send_c.at[c].reshape(32, 128),
            got_c.at[pl.ds(pl.multiple_of(col * 32, 32), 32)],
            11,
            (frame, row, c),
        )
    )
    cross_rows(got_c, send_d, 11, got_d)
    flat = got_d.reshape(256, 128)
    field = half_to_rows(
        jnp.concatenate([flat[pl.ds(0, 128, stride=2), :], flat[pl.ds(1, 128, stride=2), :]], 0),
        tab,
    )
    for x1 in range(16):
        for part in range(2):
            send_out[x1 // 2, 2 * (x1 % 2) + part] = field[
                8 * x1 : 8 * x1 + 8, 128 * part : 128 * part + 128
            ]
    got_out[col] = send_out[col]
    each_col(lambda c: send(send_out.at[c], got_out.at[col], 13, (frame, row, c)))
    wait_bytes(send_out.at[pl.ds(0, 7)], recv_sem.at[13])
    out_ref[...] = got_out[...]

    wait_bytes(object_rows.at[pl.ds(0, 7)], send_sem.at[0])
    wait_bytes(image_rows.at[pl.ds(0, 7)], send_sem.at[1])
    wait_bytes(extra, send_sem.at[2])
    for plane in range(2):
        wait_bytes(partner.at[plane], send_sem.at[3 + plane])
    wait_bytes(got_a.at[pl.ds(0, 7 * 32)], send_sem.at[5])
    wait_bytes(send_b.at[pl.ds(0, 15)], send_sem.at[6])
    wait_bytes(pencils.at[pl.ds(0, 48)], send_sem.at[7])
    wait_bytes(got_four.at[pl.ds(0, 127 * 8)], send_sem.at[8])
    wait_bytes(got_five.at[pl.ds(0, 127 * 8)], send_sem.at[9])
    wait_bytes(send_six.at[pl.ds(0, 3)], send_sem.at[10])
    wait_bytes(got_c.at[pl.ds(0, 7 * 32)], send_sem.at[11])
    wait_bytes(send_d.at[pl.ds(0, 15)], send_sem.at[12])
    wait_bytes(send_out.at[pl.ds(0, 7)], send_sem.at[13])


def tiles(block):
    rows, columns = block.shape
    return block.reshape(rows // 8, 8, columns // 128, 128).transpose(0, 2, 1, 3)


def shards(object_field, images, transfer_real, transfer_imaginary):
    made = tables()
    operands = [made[name] for name in NAMES]
    scratch = [pltpu.VMEM(table.shape, table.dtype) for table in operands]
    scratch += [
        pltpu.VMEM((2, 4, 256, 128), F32),
        pltpu.VMEM((2, 2, 256, 128), F32),
        pltpu.VMEM((2, 32, 128), F32),
        pltpu.VMEM((2, 32, 128), F32),
        pltpu.VMEM((8, 4, 8, 128), F32),
        pltpu.VMEM((8, 4, 4, 8, 128), F32),
        pltpu.VMEM((8, 2, 16, 128), F32),
        pltpu.VMEM((256, 128), F32),
        pltpu.VMEM((16, 16, 128), F32),
        pltpu.VMEM((64, 16, 128), F32),
        pltpu.VMEM((3, 2, 512, 128), F32),
        pltpu.VMEM((512, 256), BF16),
        pltpu.VMEM((512, 256), BF16),
        pltpu.VMEM((2, 1024, 128), BF16),
        pltpu.VMEM((2, 1024, 128), BF16),
        pltpu.VMEM((1024, 128), F32),
        pltpu.VMEM((1024, 128), F32),
        pltpu.VMEM((1024, 128), F32),
        pltpu.VMEM((1024, 128), F32),
        pltpu.VMEM((4, 8, 2, 16, 128), F32),
        pltpu.VMEM((4, 8, 2, 16, 128), F32),
        pltpu.VMEM((8, 2, 16, 128), F32),
        pltpu.VMEM((256, 128), F32),
        pltpu.VMEM((16, 16, 128), F32),
        pltpu.VMEM((16, 16, 128), F32),
        pltpu.VMEM((8, 4, 8, 128), F32),
        pltpu.VMEM((8, 4, 8, 128), F32),
        pltpu.SemaphoreType.DMA((len(NAMES),)),
        pltpu.SemaphoreType.DMA((4,)),
        pltpu.SemaphoreType.DMA((14,)),
        pltpu.SemaphoreType.DMA((14,)),
    ]
    anywhere = pl.BlockSpec(memory_space=pl.ANY)
    block = pl.pallas_call(
        kernel,
        out_shape=jax.ShapeDtypeStruct((8, 4, 8, 128), F32),
        in_specs=[anywhere] * (4 + len(NAMES)),
        out_specs=pl.BlockSpec(memory_space=pltpu.VMEM),
        scratch_shapes=scratch,
        compiler_params=pltpu.CompilerParams(
            collective_id=0, has_side_effects=True, vmem_limit_bytes=56 * 1024 * 1024
        ),
        name="gradient",
    )(
        tiles(object_field),
        tiles(images[0]),
        tiles(transfer_real[0]).reshape(4, 256, 128),
        tiles(transfer_imaginary[0]).reshape(4, 256, 128),
        *operands,
    )
    return block.transpose(0, 2, 1, 3).reshape(64, 512)


def solution(mesh):
    placed = (
        P("row", "col"),
        P("frame", "row", "col"),
        P("frame", ("row", "col"), None),
        P("frame", ("row", "col"), None),
    )
    return jax.shard_map(
        shards, mesh=mesh, in_specs=placed, out_specs=P(("frame", "row"), "col"), check_vma=False
    )
```

time: 504 us -> 196 us (0.39); the launches traced: 498 us -> 196 us
  blocking collectives: 212 us -> 0 us
  Pallas kernels: 0 us -> 194 us
  waiting for transfers between devices: 120 us -> 0 us
  local copies, waits for them, and re-layouts: 63.1 us -> 1.57 us
  other arithmetic: 48 us -> 0 us
  starting transfers between devices: 25.1 us -> 0 us
  matrix products: 15 us -> 0 us
  between operations: 14.8 us -> 0.01 us
    all_to_all x6 -> x0, blocking collectives: 212 us -> none  [the longest x3 167 us: deliver(): lax.all_to_all(packed, ('row', 'col'), split_axis=2, concat_axis=2, tiled...]
    pallas_call x0 -> x1, Pallas kernels: none -> 194 us  [shards(): pl.pallas_call(kernel, out_shape=jax.ShapeDtypeStruct((8, 4, 8, 128), F32...]
    all_to_all x2 -> x0, waiting for transfers between devices: 68.1 us -> none  [the longest x1 54.4 us: deliver(): lax.all_to_all(packed, ('row', 'col'), split_axis=2, concat_axis=2, tiled...]
    psum x1 -> x0, waiting for transfers between devices: 51.6 us -> none  [shards(): summed_all = lax.psum(partial_inverse, 'frame')]
    unnamed x4 -> x0, other arithmetic: 41.4 us -> none
    all_to_all x2 -> x0, starting transfers between devices: 24.8 us -> none  [the longest x1 14.6 us: deliver(): lax.all_to_all(packed, ('row', 'col'), split_axis=2, concat_axis=2, tiled...]
    another operation x10 -> x0, local copies, waits for them, and re-layouts: 18.6 us -> none
    dot_general x16 -> x0, matrix products: 15 us -> none  [the longest x8 7.6 us: transform(): jnp.einsum('p...ab,pqak->q...kb', shaped, opening, precision=highest)]
  transfers between devices with their start and end apart: 3 -> 0, of which waited for: 3 -> 0; matrix products, arithmetic and copies ran while one was open for 0% -> 0% of each run, Pallas kernels for 0% -> 0%
where the time goes in v1:
time: 196 us
  Pallas kernels  194 us (99%)
    pallas_call x1, Pallas kernels, shards(): pl.pallas_call(kernel, out_shape=jax.ShapeDtypeStruct((8, 4, 8, 128), F32...  194 us

profile of v1, /device:TPU:1, one launch (start us, length us, event | category | flops | bytes accessed | tf_op | source)
XLA Modules:
  0.0 196.0 jit_solution(13229367386991954792)
XLA Ops:
  0.0 194.5 %gradient.1 = f32[8,4,8,128]{3,2,1,0:T(8,128)} custom-call(f32[32,4,8,128]{3,2,1,0:T(8,128)} %bitcast.20, f32[32,4,8,128]{3,2,1,0:T(8,128)} %bitcast.21, f32[4,256,128]{2,1,0:T(8,128)} %bitcast.22, f32[4,256,128]{2,1,0:T(8,128)} %bitcast.23, bf16[512,128]{1,0:T(8,128)(2,1)} %constant.30.clone.refs_4_, f32[256,256]{1,0:T(8,128)} %constant.31.clone.refs_5_, ...), custom_call_target="tpu_custom_call" | custom-call | tf_op jit(solution)/shard_map/gradient/pallas_call | solution.py:644
  194.5 1.6 copy.21

commit v2 on v1

v2 whole, which is shorter than its diff:
```python
import functools
import math

import jax
import jax.numpy as jnp
import ml_dtypes
import numpy as np
from jax import lax
from jax.experimental import pallas as pl
from jax.experimental.pallas import tpu as pltpu
from jax.sharding import PartitionSpec as P

F32 = jnp.float32
BF16 = jnp.bfloat16
MESH = pl.DeviceIdType.MESH

N = 4096
DEVICES = 128


def block_of(g):
    return np.where(g < 64, 2 * g, 2 * (127 - g) + 1)


def halves(table):
    high = table.astype(np.float32).astype(ml_dtypes.bfloat16)
    low = (table - high.astype(np.float64)).astype(np.float32).astype(ml_dtypes.bfloat16)
    return high, low


def turn(numbers, length):
    angles = 2.0 * math.pi / length * (numbers % length)
    return np.cos(angles), np.sin(angles)


def vertical_forward(order):
    cosine, sine = turn(np.arange(512)[:, None] * order[None, :], 512)
    pieces = []
    for chunk in range(4):
        rows = slice(128 * chunk, 128 * chunk + 128)
        high, low = halves(np.concatenate([cosine[rows], -sine[rows]], 0))
        pieces += [high, low]
    return np.concatenate(pieces, 0)


def vertical_inverse(order):
    cosine, sine = turn(order[:, None] * np.arange(512)[None, :], 512)
    whole = np.concatenate([sine, cosine, -sine], 1)
    pieces = []
    for chunk in range(4):
        pieces += list(halves(whole[128 * chunk : 128 * chunk + 128]))
    return np.concatenate(pieces, 0)


def tables():
    made = {}
    g = np.arange(128)
    full = (4 * g[None, :] + np.arange(4)[:, None]).reshape(-1)
    f, r, c = np.meshgrid(np.arange(4), np.arange(16), np.arange(8), indexing="ij")
    made["down_object"] = vertical_forward((32 * r + 8 * f + c).reshape(-1))
    made["down_full"] = vertical_forward(full)
    made["up_full"] = vertical_inverse(full)
    made["up_gradient"] = vertical_inverse(np.arange(512))

    s, t = np.meshgrid(np.arange(16), np.arange(8), indexing="ij")
    s, t = s.reshape(-1), t.reshape(-1)
    sh, v1, sl = np.meshgrid(np.arange(2), np.arange(8), np.arange(8), indexing="ij")
    spectral_s, spectral_v = (8 * sh + sl).reshape(-1), v1.reshape(-1)
    cosine, sine = turn(t[:, None] * spectral_v[None, :], 8)
    same = (s[:, None] == spectral_s[None, :]).astype(np.float64)
    cosine, sine = cosine * same, sine * same
    made["mix_down"] = np.concatenate(halves(np.block([[cosine, -sine], [sine, cosine]])), 0)
    made["mix_up"] = np.concatenate(halves(np.block([[cosine.T, sine.T], [-sine.T, cosine.T]])), 0)
    cosine, sine = turn(np.arange(512)[:, None] * t[None, :], 4096)
    made["twist_vertical"] = np.concatenate([cosine, sine], 0).astype(np.float32)

    x1, tx = s, t
    same = (t[:, None] == tx[None, :]).astype(np.float64)
    cosine, sine = turn(s[:, None] * x1[None, :], 16)
    cosine, sine = cosine * same, sine * same
    made["open_x"] = np.concatenate(halves(np.concatenate([cosine, -sine], 0)), 0)
    scale = 1.0 / (float(N) * float(N))
    made["close_x"] = np.concatenate(halves(np.concatenate([cosine.T, -sine.T], 1) * scale), 0)
    cosine, sine = turn(s[:, None] * np.arange(256)[None, :], 4096)
    made["twist_out"] = np.concatenate([cosine, sine], 0).astype(np.float32)
    made["twist_in"] = np.concatenate([cosine.T, sine.T], 0).astype(np.float32)

    cosine, sine = turn(block_of(g)[:, None] * np.arange(256)[None, :], 256)
    alternate = np.zeros((16, 512))
    alternate[0, :256] = 1.0 - 2.0 * (np.arange(256) % 2)
    whole = np.block([[cosine, sine], [-sine, cosine]])
    made["across"] = np.concatenate(halves(np.concatenate([whole, alternate], 0)), 0)
    cosine, sine = turn(np.arange(256)[:, None] * block_of(g)[None, :], 256)
    made["back_x"] = np.concatenate(halves(np.block([[cosine, -sine], [sine, cosine]])), 0)

    choose = np.zeros((3, 384, 512))
    for kind in range(3):
        for row in range(128):
            slot, v = spectral_s[row], spectral_v[row]

            def own(number):
                return (number // 8) * 64 + v * 8 + number % 8

            def got(number):
                return 256 + (number // 8) * 64 + v * 8 + number % 8

            extra = 384 + v
            if kind == 2:
                plus, minus = got(slot), own(16 - slot)
            else:
                plus, minus = own(slot), (extra if slot == 0 else got(16 - slot))
            if kind == 0 and slot == 0:
                choose[kind, row, plus] = 1.0
                choose[kind, 128 + row, minus] = 1.0
            else:
                for part, sign in ((0, 1.0), (128, 1.0), (256, -1.0)):
                    choose[kind, part + row, plus] = 1.0
                    choose[kind, part + row, minus] = sign
    made["choose"] = choose.astype(ml_dtypes.bfloat16)
    return made


def product(left, right):
    return lax.dot_general(left, right, (((1,), (0,)), ((), ())), preferred_element_type=F32)


def product_turned(left, right):
    return lax.dot_general(left, right, (((1,), (1,)), ((), ())), preferred_element_type=F32)


def split(values):
    high = values.astype(BF16)
    return high, (values - high.astype(F32)).astype(BF16)


def table_first(table, high, low, dot):
    rows = table.shape[0] // 2
    both = dot(table, high)
    return both[:rows] + (both[rows:] + dot(table[:rows], low))


def table_last(values, table):
    depth = table.shape[0] // 2
    rows = values.shape[0]
    high, low = split(values)
    both = product(jnp.concatenate([high, low], 0), table[:depth])
    return both[:rows] + (both[rows:] + product(high, table[depth:]))


def rows_to_half(fields, tab):
    opened = table_first(tab["open_x"][...], *split(jnp.concatenate(fields, 1)), product)
    cosine, sine = tab["twist_out"][:128, :], tab["twist_out"][128:, :]
    turned = []
    for number in range(len(fields)):
        part = slice(256 * number, 256 * number + 256)
        real, imaginary = opened[:128, part], opened[128:, part]
        turned.append(
            jnp.concatenate(
                [real * cosine + imaginary * sine, imaginary * cosine - real * sine], 1
            )
        )
    out = table_first(tab["across"][...], *split(jnp.concatenate(turned, 0)), product_turned)
    row = lax.broadcasted_iota(jnp.int32, (128, 128), 0)
    lane = lax.broadcasted_iota(jnp.int32, (128, 128), 1)
    shared = (row == 0) & (lane < 8)
    pairs = []
    for number in range(len(fields)):
        part = slice(128 * number, 128 * number + 128)
        extra = jnp.where(shared, out[256:257, part], 0.0)
        pairs.append((out[:128, part], out[128:256, part] + extra))
    return pairs


def half_to_rows(planes, tab):
    back = table_first(tab["back_x"][...], *split(jnp.concatenate(planes, 1)), product)
    lane = lax.broadcasted_iota(jnp.int32, (256, 128), 1)
    number = lax.broadcasted_iota(jnp.int32, (256, 128), 0)
    cosine, sine = tab["twist_in"][:256, :], tab["twist_in"][256:, :]
    fields = []
    for which, plane in enumerate(planes):
        part = slice(128 * which, 128 * which + 128)
        shared = jnp.where(lane < 8, plane[128:129], 0.0)
        real = back[:256, part] + jnp.where(number % 2 == 0, shared, -shared)
        imaginary = back[256:, part]
        turned = jnp.concatenate(
            [real * cosine - imaginary * sine, real * sine + imaginary * cosine], 1
        )
        fields.append(table_first(tab["close_x"][...], *split(turned), product_turned))
    return fields


def down_chunk(table, high, low, cosine, sine, tab):
    opened = table_first(table, high, low, product)
    real, imaginary = opened[:128], opened[128:]
    cosine = jnp.concatenate([cosine, cosine], 1)
    sine = jnp.concatenate([sine, sine], 1)
    turned_real = real * cosine + imaginary * sine
    turned_imaginary = imaginary * cosine - real * sine
    stacked = jnp.concatenate(
        [
            jnp.concatenate([turned_real[:, :128], turned_imaginary[:, :128]], 1),
            jnp.concatenate([turned_real[:, 128:], turned_imaginary[:, 128:]], 1),
        ],
        0,
    )
    return table_last(stacked, tab["mix_down"][...])


def up_chunk(mixed, cosine, sine, tab, weights, conjugate):
    ar, ai = mixed[:128, :128], mixed[:128, 128:]
    br, bi = mixed[128:, :128], mixed[128:, 128:]
    (s1r, s1i), (s2r, s2i), (dr, di) = weights
    if conjugate:
        s1i, s2i, di = -s1i, -s2i, -di
    ur = s1r * ar - s1i * ai - (dr * bi + di * br)
    ui = s1r * ai + s1i * ar + (dr * br - di * bi)
    vr = dr * ar - di * ai - (s2r * bi + s2i * br)
    vi = dr * ai + di * ar + (s2r * br - s2i * bi)
    stacked = jnp.concatenate(
        [jnp.concatenate([ur, ui], 1), jnp.concatenate([vr, vi], 1)], 0
    )
    mixed = table_last(stacked, tab["mix_up"][...])
    cosine = jnp.concatenate([cosine, cosine], 0)
    sine = jnp.concatenate([sine, sine], 0)
    real, imaginary = mixed[:, :128], mixed[:, 128:]
    return real * cosine - imaginary * sine, real * sine + imaginary * cosine


NAMES = (
    "open_x",
    "twist_out",
    "across",
    "down_object",
    "twist_vertical",
    "mix_down",
    "choose",
    "mix_up",
    "up_full",
    "back_x",
    "twist_in",
    "close_x",
    "down_full",
    "up_gradient",
)


def kernel(*refs):
    object_ref, images_ref, real_ref, imaginary_ref = refs[:4]
    sources = refs[4 : 4 + len(NAMES)]
    out_ref = refs[4 + len(NAMES)]
    rest = refs[5 + len(NAMES) :]
    tab = dict(zip(NAMES, rest[: len(NAMES)]))
    (
        transfer,
        partner,
        extra_send,
        extra,
        object_rows,
        image_rows,
        send_a,
        pencils,
        middle,
        weight,
        split_high,
        split_low,
        back_high,
        back_low,
        send_four,
        got_four,
        send_five,
        got_five,
        send_six,
        got_six,
        send_c,
        got_d,
        send_out,
        got_out,
        table_sem,
        local_sem,
        send_sem,
        recv_sem,
    ) = rest[len(NAMES) :]

    frame, row, col = lax.axis_index("frame"), lax.axis_index("row"), lax.axis_index("col")
    me = row * 8 + col

    loads = {
        name: pltpu.make_async_copy(source, tab[name], table_sem.at[number])
        for number, (name, source) in enumerate(zip(NAMES, sources))
    }

    def need(*names):
        for name in names:
            loads[name].wait()

    transfer_loads = [
        pltpu.make_async_copy(real_ref, transfer.at[0], local_sem.at[0]),
        pltpu.make_async_copy(imaginary_ref, transfer.at[1], local_sem.at[1]),
    ]
    object_load = pltpu.make_async_copy(
        object_ref.at[8 * frame + col], object_rows.at[col], local_sem.at[2]
    )
    images_load = pltpu.make_async_copy(
        images_ref.at[pl.ds(4 * col, 4)], image_rows.at[col], local_sem.at[3]
    )
    for load in transfer_loads:
        load.start()
    object_load.start()
    images_load.start()
    for name in NAMES:
        loads[name].start()

    barrier = pltpu.get_barrier_semaphore()

    columns = [lax.rem(col + number, 8) for number in range(8)]

    def each_peer(body):
        for c in columns[1:]:
            body(row, c)

        def step(number, carry):
            r = lax.rem(row + number, 16)
            for c in columns:
                body(r, c)
            return carry

        lax.fori_loop(1, 16, step, 0)

    opposite = 127 - me
    is_end = 1 - (lax.rem(me, 64) + 63) // 64
    beyond = 128 - me - 64 * is_end
    mirror = (frame, opposite // 8, lax.rem(opposite, 8))
    after = (frame, beyond // 8, lax.rem(beyond, 8))

    def greet(device):
        pl.semaphore_signal(barrier, inc=1, device_id=device, device_id_type=MESH)

    greet(mirror)
    greet(after)
    for c in columns[1:]:
        greet((frame, row, c))

    def greet_row(number, carry):
        greet((frame, lax.rem(row + number, 16), col))
        return carry

    lax.fori_loop(1, 16, greet_row, 0)
    for step in range(1, 4):
        greet((lax.rem(frame + step, 4), row, col))
    pl.semaphore_wait(barrier, 2 + 7 + 15 + 3)

    def send(source, target, phase, device):
        pltpu.make_async_remote_copy(
            src_ref=source,
            dst_ref=target,
            send_sem=send_sem.at[phase],
            recv_sem=recv_sem.at[phase],
            device_id=device,
            device_id_type=MESH,
        ).start()

    def wait_bytes(like, semaphore):
        pltpu.make_async_copy(like, like, semaphore).wait()

    def each_col(body):
        for c in columns[1:]:
            body(c)

    def each_frame(body):
        for number in range(1, 4):
            body(lax.rem(frame + number, 4))

    def block(number, size):
        return pl.ds(pl.multiple_of(number * size, size), size)

    each_col(
        lambda c: send(
            object_ref.at[8 * frame + c], object_rows.at[col], 0, (frame, row, c)
        )
    )
    for load in transfer_loads:
        load.wait()
    for plane in range(2):
        extra_send[plane] = transfer[plane, 0, pl.ds(0, 32, stride=8), :]
    def send_partner(number):
        plane, a, part = number // 8, lax.rem(number // 4, 2), lax.rem(number, 4)
        rows = block(part, 64)
        send(transfer.at[plane, 2 + a, rows], partner.at[plane, a, rows], 3, mirror)

    def send_image(c):
        send(images_ref.at[pl.ds(4 * c, 4)], image_rows.at[col], 1, (frame, row, c))

    for number in range(3):
        send_partner(number)

    def field_of(read):
        return jnp.concatenate(
            [
                jnp.concatenate([read(x1 // 2, 2 * (x1 % 2) + part) for x1 in range(16)], 0)
                for part in range(2)
            ],
            1,
        )

    def to_all(source, target, size, phase):
        target[block(me, size), :] = source[block(me, size), :]
        own = block(me, size)
        each_peer(
            lambda r, c: send(
                source.at[block(r * 8 + c, size)], target.at[own], phase, (frame, r, c)
            )
        )

    object_load.wait()
    wait_bytes(object_rows.at[pl.ds(0, 7)], recv_sem.at[0])
    need("open_x", "twist_out", "across")
    planes = rows_to_half([field_of(lambda c, k: object_rows[c, k])], tab)[0]
    for plane in range(2):
        send_a[pl.ds(plane, 128, stride=2), :] = planes[plane]
    quarter = pencils.at[block(frame, 256)]
    quarter[block(me, 2), :] = send_a[block(me, 2), :]

    def send_pencil(r, c):
        send(send_a.at[block(r * 8 + c, 2)], quarter.at[block(me, 2)], 5, (frame, r, c))

    for c in columns[1:]:
        send_pencil(row, c)

    def some_rows(step, carry):
        for number in range(1, 6):
            for c in columns:
                send_pencil(lax.rem(row + 5 * step + number, 16), c)
        send_partner(3 + step)
        return carry

    lax.fori_loop(0, 3, some_rows, 0)
    send(extra_send, extra, 2, after)
    for number in range(6, 16):
        send_partner(number)
        if number >= 9:
            send_image(columns[number - 8])
    wait_bytes(send_a.at[pl.ds(0, 254)], recv_sem.at[5])
    each_frame(lambda f: send(quarter, quarter, 7, (f, row, col)))
    wait_bytes(pencils.at[pl.ds(0, 768)], recv_sem.at[7])

    def turns(number):
        return (
            tab["twist_vertical"][pl.ds(128 * number, 128), :],
            tab["twist_vertical"][pl.ds(512 + 128 * number, 128), :],
        )

    def down(name, number):
        return down_chunk(
            tab[name][pl.ds(512 * number, 512), :],
            split_high[...],
            split_low[...],
            *turns(number),
            tab,
        )

    def up(mixed, number, conjugate):
        rows = pl.ds(128 * number, 128)
        weights = [(weight[k, 0, rows, :], weight[k, 1, rows, :]) for k in range(3)]
        planes = up_chunk(mixed, *turns(number), tab, weights, conjugate)
        for plane, values in enumerate(planes):
            high, low = split(values)
            for which in range(2):
                part = slice(128 * which, 128 * which + 128)
                at = pl.ds(512 * plane + 128 * number, 128)
                back_high[which, at, :] = high[part]
                back_low[which, at, :] = low[part]

    for plane in range(2):
        high, low = split(pencils[pl.ds(plane, 512, stride=2), :])
        split_high[:, 128 * plane : 128 * plane + 128] = high
        split_low[:, 128 * plane : 128 * plane + 128] = low
    need("down_object", "twist_vertical", "mix_down")
    for number in range(4):
        middle[number] = down("down_object", number)

    wait_bytes(extra, recv_sem.at[2])
    wait_bytes(partner, recv_sem.at[3])
    need("choose")
    kind = (me + 127) // 128 + me // 64
    for part in range(4):
        blocks = []
        for plane in range(2):
            rows = [
                transfer[plane, a, pl.ds((4 * v + part) * 8, 8), :]
                for a in range(4)
                for v in range(8)
            ]
            rows += [
                partner[plane, a, pl.ds((4 * v + part) * 8, 8), :]
                for a in range(2)
                for v in range(8)
            ]
            rows += [extra[plane, pl.ds(part, 8, stride=4), :], jnp.zeros((120, 128), F32)]
            blocks.append(jnp.concatenate(rows, 0))
        gathered = jnp.concatenate(blocks, 1)
        first = gathered.astype(BF16)
        left = gathered - first.astype(F32)
        second = left.astype(BF16)
        third = (left - second.astype(F32)).astype(BF16)
        chosen = tab["choose"][kind]
        picked = product(chosen, first) + (product(chosen, second) + product(chosen, third))
        for number in range(3):
            for plane in range(2):
                weight[number, plane, pl.ds(128 * part, 128), :] = picked[
                    128 * number : 128 * number + 128, 128 * plane : 128 * plane + 128
                ].T

    def return_chunk(name, number):
        table = tab[name][block(number, 256), :]
        real = table_first(table[:, 512:], back_high[0], back_low[0], product)
        imaginary = table_first(table[:, :1024], back_high[1], back_low[1], product)
        return real, imaginary

    need("mix_up")
    for number in range(4):
        up(middle[number], number, False)
    need("up_full")
    for number in range(4):
        real, imaginary = return_chunk("up_full", number)
        send_four[pl.ds(number, 128, stride=8), :] = real
        send_four[pl.ds(4 + number, 128, stride=8), :] = imaginary
    to_all(send_four, got_four, 8, 8)

    images_load.wait()
    wait_bytes(image_rows.at[pl.ds(0, 7)], recv_sem.at[1])
    need("back_x", "twist_in", "close_x")
    wait_bytes(got_four.at[pl.ds(0, 127 * 8)], recv_sem.at[8])
    for first in (0, 2):
        both = (first, first + 1)
        modelled = half_to_rows(
            [
                jnp.concatenate(
                    [
                        got_four[pl.ds(number, 128, stride=8), :],
                        got_four[pl.ds(4 + number, 128, stride=8), :],
                    ],
                    0,
                )
                for number in both
            ],
            tab,
        )
        weighted = []
        for number, model in zip(both, modelled):
            images = field_of(lambda c, k: image_rows[c, number, k])
            weighted.append((model - images) / (0.5 + jnp.abs(images)))
        for number, planes in zip(both, rows_to_half(weighted, tab)):
            for plane in range(2):
                send_five[pl.ds(4 * plane + number, 128, stride=8), :] = planes[plane]
    to_all(send_five, got_five, 8, 9)

    need("down_full", "up_gradient")
    wait_bytes(got_five.at[pl.ds(0, 127 * 8)], recv_sem.at[9])
    for plane in range(2):
        for number in range(4):
            high, low = split(got_five[pl.ds(4 * plane + number, 128, stride=8), :])
            at = (slice(128 * number, 128 * number + 128), slice(128 * plane, 128 * plane + 128))
            split_high[at] = high
            split_low[at] = low
    for number in range(4):
        up(down("down_full", number), number, True)

    near = row // 8
    parts = [block(near, 128), block(1 - near, 128)]
    for step in (2, 1, 3, 0):
        f = lax.rem(frame + step, 4)
        planes = return_chunk("up_gradient", f)
        target = got_six if step == 0 else send_six
        for plane in range(2):
            target[f, pl.ds(plane, 128, stride=2), :] = planes[plane]
        if step > 0:
            send(send_six.at[f, parts[0]], got_six.at[frame, parts[0]], 4, (f, row, col))
    for step in (2, 1, 3):
        f = lax.rem(frame + step, 4)
        send(send_six.at[f, parts[1]], got_six.at[frame, parts[1]], 10, (f, row, col))
    for half in range(2):
        wait_bytes(send_six.at[pl.ds(0, 3), pl.ds(0, 128)], recv_sem.at[4 if half == 0 else 10])
        pieces = [got_six[f, parts[half], :] for f in range(4)]
        send_c[parts[half], :] = (pieces[0] + pieces[1]) + (pieces[2] + pieces[3])
        first = 8 * near if half == 0 else 8 - 8 * near

        def send_quarter(r, c):
            send(send_c.at[block(r * 8 + c, 2)], got_d.at[block(me, 2)], 11, (frame, r, c))

        def some_rows(number, carry):
            for c in columns:
                send_quarter(first + lax.rem(row + number, 8), c)
            return carry

        if half == 0:
            got_d[block(me, 2), :] = send_c[block(me, 2), :]
            for c in columns[1:]:
                send_quarter(row, c)
        lax.fori_loop(1 - half, 8, some_rows, 0)
    wait_bytes(send_c.at[pl.ds(0, 254)], recv_sem.at[11])
    field = half_to_rows(
        [jnp.concatenate([got_d[pl.ds(0, 128, stride=2), :], got_d[pl.ds(1, 128, stride=2), :]], 0)],
        tab,
    )[0]
    for x1 in range(16):
        for part in range(2):
            send_out[x1 // 2, 2 * (x1 % 2) + part] = field[
                8 * x1 : 8 * x1 + 8, 128 * part : 128 * part + 128
            ]
    got_out[col] = send_out[col]
    each_col(lambda c: send(send_out.at[c], got_out.at[col], 13, (frame, row, c)))
    wait_bytes(send_out.at[pl.ds(0, 7)], recv_sem.at[13])
    out_ref[...] = got_out[...]

    wait_bytes(object_rows.at[pl.ds(0, 7)], send_sem.at[0])
    wait_bytes(image_rows.at[pl.ds(0, 7)], send_sem.at[1])
    wait_bytes(extra, send_sem.at[2])
    wait_bytes(partner, send_sem.at[3])
    wait_bytes(send_a.at[pl.ds(0, 254)], send_sem.at[5])
    wait_bytes(pencils.at[pl.ds(0, 768)], send_sem.at[7])
    wait_bytes(got_four.at[pl.ds(0, 127 * 8)], send_sem.at[8])
    wait_bytes(got_five.at[pl.ds(0, 127 * 8)], send_sem.at[9])
    wait_bytes(send_six.at[pl.ds(0, 3), pl.ds(0, 128)], send_sem.at[4])
    wait_bytes(send_six.at[pl.ds(0, 3), pl.ds(0, 128)], send_sem.at[10])
    wait_bytes(send_c.at[pl.ds(0, 254)], send_sem.at[11])
    wait_bytes(send_out.at[pl.ds(0, 7)], send_sem.at[13])


def tiles(block):
    rows, columns = block.shape
    return block.reshape(rows // 8, 8, columns // 128, 128).transpose(0, 2, 1, 3)


def shards(object_field, images, transfer_real, transfer_imaginary):
    made = tables()
    operands = [made[name] for name in NAMES]
    scratch = [pltpu.VMEM(table.shape, table.dtype) for table in operands]
    scratch += [
        pltpu.VMEM((2, 4, 256, 128), F32),
        pltpu.VMEM((2, 2, 256, 128), F32),
        pltpu.VMEM((2, 32, 128), F32),
        pltpu.VMEM((2, 32, 128), F32),
        pltpu.VMEM((8, 4, 8, 128), F32),
        pltpu.VMEM((8, 4, 4, 8, 128), F32),
        pltpu.VMEM((256, 128), F32),
        pltpu.VMEM((1024, 128), F32),
        pltpu.VMEM((4, 256, 256), F32),
        pltpu.VMEM((3, 2, 512, 128), F32),
        pltpu.VMEM((512, 256), BF16),
        pltpu.VMEM((512, 256), BF16),
        pltpu.VMEM((2, 1024, 128), BF16),
        pltpu.VMEM((2, 1024, 128), BF16),
        pltpu.VMEM((1024, 128), F32),
        pltpu.VMEM((1024, 128), F32),
        pltpu.VMEM((1024, 128), F32),
        pltpu.VMEM((1024, 128), F32),
        pltpu.VMEM((4, 256, 128), F32),
        pltpu.VMEM((4, 256, 128), F32),
        pltpu.VMEM((256, 128), F32),
        pltpu.VMEM((256, 128), F32),
        pltpu.VMEM((8, 4, 8, 128), F32),
        pltpu.VMEM((8, 4, 8, 128), F32),
        pltpu.SemaphoreType.DMA((len(NAMES),)),
        pltpu.SemaphoreType.DMA((4,)),
        pltpu.SemaphoreType.DMA((14,)),
        pltpu.SemaphoreType.DMA((14,)),
    ]
    anywhere = pl.BlockSpec(memory_space=pl.ANY)
    block = pl.pallas_call(
        kernel,
        out_shape=jax.ShapeDtypeStruct((8, 4, 8, 128), F32),
        in_specs=[anywhere] * (4 + len(NAMES)),
        out_specs=pl.BlockSpec(memory_space=pltpu.VMEM),
        scratch_shapes=scratch,
        compiler_params=pltpu.CompilerParams(
            collective_id=0, has_side_effects=True, vmem_limit_bytes=56 * 1024 * 1024
        ),
        name="gradient",
    )(
        tiles(object_field),
        tiles(images[0]),
        tiles(transfer_real[0]).reshape(4, 256, 128),
        tiles(transfer_imaginary[0]).reshape(4, 256, 128),
        *operands,
    )
    return block.transpose(0, 2, 1, 3).reshape(64, 512)


def solution(mesh):
    placed = (
        P("row", "col"),
        P("frame", "row", "col"),
        P("frame", ("row", "col"), None),
        P("frame", ("row", "col"), None),
    )
    return jax.shard_map(
        shards, mesh=mesh, in_specs=placed, out_specs=P(("frame", "row"), "col"), check_vma=False
    )
```

time: 196 us -> 169 us (0.86)
  Pallas kernels: 194 us -> 168 us
    pallas_call x1, Pallas kernels: 194 us -> 168 us  [shards(): pl.pallas_call(kernel, out_shape=jax.ShapeDtypeStruct((8, 4, 8, 128), F32...]
where the time goes in v2:
time: 169 us
  Pallas kernels  168 us (99%)
    pallas_call x1, Pallas kernels, shards(): pl.pallas_call(kernel, out_shape=jax.ShapeDtypeStruct((8, 4, 8, 128), F32...  168 us

profile of v2, /device:TPU:1, one launch (start us, length us, event | category | flops | bytes accessed | tf_op | source)
XLA Modules:
  0.0 169.2 jit_solution(1676809626018391519)
XLA Ops:
  0.0 167.6 %gradient.1 = f32[8,4,8,128]{3,2,1,0:T(8,128)} custom-call(f32[32,4,8,128]{3,2,1,0:T(8,128)} %bitcast.20, f32[32,4,8,128]{3,2,1,0:T(8,128)} %bitcast.21, f32[4,256,128]{2,1,0:T(8,128)} %bitcast.22, f32[4,256,128]{2,1,0:T(8,128)} %bitcast.23, bf16[512,128]{1,0:T(8,128)(2,1)} %constant.28.clone.refs_4_, f32[256,256]{1,0:T(8,128)} %constant.29.clone.refs_5_, ...), custom_call_target="tpu_custom_call" | custom-call | tf_op jit(solution)/shard_map/gradient/pallas_call | solution.py:669
  167.6 1.6 copy.20

commit v3 on v2

--- a/solution.py
+++ b/solution.py
@@ -189,8 +189,7 @@
     return fields
 
 
-def down_chunk(table, high, low, cosine, sine, tab):
-    opened = table_first(table, high, low, product)
+def down_chunk(opened, cosine, sine, tab):
     real, imaginary = opened[:128], opened[128:]
     cosine = jnp.concatenate([cosine, cosine], 1)
     sine = jnp.concatenate([sine, sine], 1)
@@ -315,16 +314,17 @@
     columns = [lax.rem(col + number, 8) for number in range(8)]
 
     def each_peer(body):
+        for first, last in ((8, 12), (12, 16), (4, 8), (1, 4)):
+
+            def step(number, carry):
+                r = lax.rem(row + number, 16)
+                for c in columns:
+                    body(r, c)
+                return carry
+
+            lax.fori_loop(first, last, step, 0)
         for c in columns[1:]:
             body(row, c)
-
-        def step(number, carry):
-            r = lax.rem(row + number, 16)
-            for c in columns:
-                body(r, c)
-            return carry
-
-        lax.fori_loop(1, 16, step, 0)
 
     opposite = 127 - me
     is_end = 1 - (lax.rem(me, 64) + 63) // 64
@@ -390,7 +390,7 @@
     def send_image(c):
         send(images_ref.at[pl.ds(4 * c, 4)], image_rows.at[col], 1, (frame, row, c))
 
-    for number in range(3):
+    for number in range(6):
         send_partner(number)
 
     def field_of(read):
@@ -423,16 +423,14 @@
     def send_pencil(r, c):
         send(send_a.at[block(r * 8 + c, 2)], quarter.at[block(me, 2)], 5, (frame, r, c))
 
+    def some_rows(step, carry):
+        for number in range(5):
+            for c in columns:
+                send_pencil(lax.rem(row + 1 + lax.rem(6 + 5 * step + number, 15), 16), c)
+        return carry
+
     for c in columns[1:]:
         send_pencil(row, c)
-
-    def some_rows(step, carry):
-        for number in range(1, 6):
-            for c in columns:
-                send_pencil(lax.rem(row + 5 * step + number, 16), c)
-        send_partner(3 + step)
-        return carry
-
     lax.fori_loop(0, 3, some_rows, 0)
     send(extra_send, extra, 2, after)
     for number in range(6, 16):
@@ -449,13 +447,9 @@
             tab["twist_vertical"][pl.ds(512 + 128 * number, 128), :],
         )
 
-    def down(name, number):
-        return down_chunk(
-            tab[name][pl.ds(512 * number, 512), :],
-            split_high[...],
-            split_low[...],
-            *turns(number),
-            tab,
+    def opened(name, number, rows):
+        return table_first(
+            tab[name][pl.ds(512 * number, 512), rows], split_high[rows], split_low[rows], product
         )
 
     def up(mixed, number, conjugate):
@@ -476,7 +470,9 @@
         split_low[:, 128 * plane : 128 * plane + 128] = low
     need("down_object", "twist_vertical", "mix_down")
     for number in range(4):
-        middle[number] = down("down_object", number)
+        middle[number] = down_chunk(
+            opened("down_object", number, slice(0, 512)), *turns(number), tab
+        )
 
     wait_bytes(extra, recv_sem.at[2])
     wait_bytes(partner, recv_sem.at[3])
@@ -520,50 +516,58 @@
     for number in range(4):
         up(middle[number], number, False)
     need("up_full")
-    for number in range(4):
-        real, imaginary = return_chunk("up_full", number)
-        send_four[pl.ds(number, 128, stride=8), :] = real
-        send_four[pl.ds(4 + number, 128, stride=8), :] = imaginary
-    to_all(send_four, got_four, 8, 8)
+    for half in range(2):
+        for number in range(2):
+            planes = return_chunk("up_full", 2 * half + number)
+            for plane in range(2):
+                send_four[half, pl.ds(2 * plane + number, 128, stride=4), :] = planes[plane]
+        if half == 1:
+            wait_bytes(got_four.at[0, pl.ds(0, 127 * 4)], send_sem.at[8])
+        to_all(send_four.at[half], got_four.at[half], 4, 8 + half)
 
     images_load.wait()
     wait_bytes(image_rows.at[pl.ds(0, 7)], recv_sem.at[1])
     need("back_x", "twist_in", "close_x")
-    wait_bytes(got_four.at[pl.ds(0, 127 * 8)], recv_sem.at[8])
-    for first in (0, 2):
-        both = (first, first + 1)
+    for half in range(2):
+        wait_bytes(got_four.at[half, pl.ds(0, 127 * 4)], recv_sem.at[8 + half])
         modelled = half_to_rows(
             [
                 jnp.concatenate(
                     [
-                        got_four[pl.ds(number, 128, stride=8), :],
-                        got_four[pl.ds(4 + number, 128, stride=8), :],
+                        got_four[half, pl.ds(number, 128, stride=4), :],
+                        got_four[half, pl.ds(2 + number, 128, stride=4), :],
                     ],
                     0,
                 )
-                for number in both
+                for number in range(2)
             ],
             tab,
         )
         weighted = []
-        for number, model in zip(both, modelled):
-            images = field_of(lambda c, k: image_rows[c, number, k])
+        for number, model in enumerate(modelled):
+            images = field_of(lambda c, k: image_rows[c, 2 * half + number, k])
             weighted.append((model - images) / (0.5 + jnp.abs(images)))
-        for number, planes in zip(both, rows_to_half(weighted, tab)):
+        for number, planes in enumerate(rows_to_half(weighted, tab)):
             for plane in range(2):
-                send_five[pl.ds(4 * plane + number, 128, stride=8), :] = planes[plane]
-    to_all(send_five, got_five, 8, 9)
+                send_five[half, pl.ds(2 * plane + number, 128, stride=4), :] = planes[plane]
+        to_all(send_five.at[half], got_five.at[half], 4, 14 + half)
 
     need("down_full", "up_gradient")
-    wait_bytes(got_five.at[pl.ds(0, 127 * 8)], recv_sem.at[9])
-    for plane in range(2):
-        for number in range(4):
-            high, low = split(got_five[pl.ds(4 * plane + number, 128, stride=8), :])
-            at = (slice(128 * number, 128 * number + 128), slice(128 * plane, 128 * plane + 128))
-            split_high[at] = high
-            split_low[at] = low
+    for half in range(2):
+        wait_bytes(got_five.at[half, pl.ds(0, 127 * 4)], recv_sem.at[14 + half])
+        for plane in range(2):
+            for number in range(2):
+                high, low = split(got_five[half, pl.ds(2 * plane + number, 128, stride=4), :])
+                first = 256 * half + 128 * number
+                at = (slice(first, first + 128), slice(128 * plane, 128 * plane + 128))
+                split_high[at] = high
+                split_low[at] = low
+        if half == 0:
+            for number in range(4):
+                middle[number] = opened("down_full", number, slice(0, 256))
     for number in range(4):
-        up(down("down_full", number), number, True)
+        whole = middle[number] + opened("down_full", number, slice(256, 512))
+        up(down_chunk(whole, *turns(number), tab), number, True)
 
     near = row // 8
     parts = [block(near, 128), block(1 - near, 128)]
@@ -618,8 +622,9 @@
     wait_bytes(partner, send_sem.at[3])
     wait_bytes(send_a.at[pl.ds(0, 254)], send_sem.at[5])
     wait_bytes(pencils.at[pl.ds(0, 768)], send_sem.at[7])
-    wait_bytes(got_four.at[pl.ds(0, 127 * 8)], send_sem.at[8])
-    wait_bytes(got_five.at[pl.ds(0, 127 * 8)], send_sem.at[9])
+    wait_bytes(got_four.at[1, pl.ds(0, 127 * 4)], send_sem.at[9])
+    for half in range(2):
+        wait_bytes(got_five.at[half, pl.ds(0, 127 * 4)], send_sem.at[14 + half])
     wait_bytes(send_six.at[pl.ds(0, 3), pl.ds(0, 128)], send_sem.at[4])
     wait_bytes(send_six.at[pl.ds(0, 3), pl.ds(0, 128)], send_sem.at[10])
     wait_bytes(send_c.at[pl.ds(0, 254)], send_sem.at[11])
@@ -650,10 +655,10 @@
         pltpu.VMEM((512, 256), BF16),
         pltpu.VMEM((2, 1024, 128), BF16),
         pltpu.VMEM((2, 1024, 128), BF16),
-        pltpu.VMEM((1024, 128), F32),
-        pltpu.VMEM((1024, 128), F32),
-        pltpu.VMEM((1024, 128), F32),
-        pltpu.VMEM((1024, 128), F32),
+        pltpu.VMEM((2, 512, 128), F32),
+        pltpu.VMEM((2, 512, 128), F32),
+        pltpu.VMEM((2, 512, 128), F32),
+        pltpu.VMEM((2, 512, 128), F32),
         pltpu.VMEM((4, 256, 128), F32),
         pltpu.VMEM((4, 256, 128), F32),
         pltpu.VMEM((256, 128), F32),
@@ -662,8 +667,8 @@
         pltpu.VMEM((8, 4, 8, 128), F32),
         pltpu.SemaphoreType.DMA((len(NAMES),)),
         pltpu.SemaphoreType.DMA((4,)),
-        pltpu.SemaphoreType.DMA((14,)),
-        pltpu.SemaphoreType.DMA((14,)),
+        pltpu.SemaphoreType.DMA((16,)),
+        pltpu.SemaphoreType.DMA((16,)),
     ]
     anywhere = pl.BlockSpec(memory_space=pl.ANY)
     block = pl.pallas_call(

time: 169 us -> 158 us (0.935)
  Pallas kernels: 168 us -> 156 us
    pallas_call x1, Pallas kernels: 168 us -> 156 us  [shards(): pl.pallas_call(kernel, out_shape=jax.ShapeDtypeStruct((8, 4, 8, 128), F32...]
where the time goes in v3:
time: 158 us
  Pallas kernels  156 us (99%)
    pallas_call x1, Pallas kernels, shards(): pl.pallas_call(kernel, out_shape=jax.ShapeDtypeStruct((8, 4, 8, 128), F32...  156 us

profile of v3, /device:TPU:1, one launch (start us, length us, event | category | flops | bytes accessed | tf_op | source)
XLA Modules:
  0.0 157.8 jit_solution(16358247450207554096)
XLA Ops:
  0.0 156.2 %gradient.1 = f32[8,4,8,128]{3,2,1,0:T(8,128)} custom-call(f32[32,4,8,128]{3,2,1,0:T(8,128)} %bitcast.20, f32[32,4,8,128]{3,2,1,0:T(8,128)} %bitcast.21, f32[4,256,128]{2,1,0:T(8,128)} %bitcast.22, f32[4,256,128]{2,1,0:T(8,128)} %bitcast.23, bf16[512,128]{1,0:T(8,128)(2,1)} %constant.28.clone.refs_4_, f32[256,256]{1,0:T(8,128)} %constant.29.clone.refs_5_, ...), custom_call_target="tpu_custom_call" | custom-call | tf_op jit(solution)/shard_map/gradient/pallas_call | solution.py:674
  156.3 1.6 copy.20

commit v4 on v3

--- a/solution.py
+++ b/solution.py
@@ -282,6 +282,30 @@
 
     frame, row, col = lax.axis_index("frame"), lax.axis_index("row"), lax.axis_index("col")
     me = row * 8 + col
+    barrier = pltpu.get_barrier_semaphore()
+    columns = [lax.rem(col + number, 8) for number in range(8)]
+
+    opposite = 127 - me
+    is_end = 1 - (lax.rem(me, 64) + 63) // 64
+    beyond = 128 - me - 64 * is_end
+    mirror = (frame, opposite // 8, lax.rem(opposite, 8))
+    after = (frame, beyond // 8, lax.rem(beyond, 8))
+
+    def greet(device):
+        pl.semaphore_signal(barrier, inc=1, device_id=device, device_id_type=MESH)
+
+    greet(mirror)
+    greet(after)
+    for c in columns[1:]:
+        greet((frame, row, c))
+
+    def greet_row(number, carry):
+        greet((frame, lax.rem(row + number, 16), col))
+        return carry
+
+    lax.fori_loop(1, 16, greet_row, 0)
+    for step in range(1, 4):
+        greet((lax.rem(frame + step, 4), row, col))
 
     loads = {
         name: pltpu.make_async_copy(source, tab[name], table_sem.at[number])
@@ -309,9 +333,6 @@
     for name in NAMES:
         loads[name].start()
 
-    barrier = pltpu.get_barrier_semaphore()
-
-    columns = [lax.rem(col + number, 8) for number in range(8)]
 
     def each_peer(body):
         for first, last in ((8, 12), (12, 16), (4, 8), (1, 4)):
@@ -326,27 +347,6 @@
         for c in columns[1:]:
             body(row, c)
 
-    opposite = 127 - me
-    is_end = 1 - (lax.rem(me, 64) + 63) // 64
-    beyond = 128 - me - 64 * is_end
-    mirror = (frame, opposite // 8, lax.rem(opposite, 8))
-    after = (frame, beyond // 8, lax.rem(beyond, 8))
-
-    def greet(device):
-        pl.semaphore_signal(barrier, inc=1, device_id=device, device_id_type=MESH)
-
-    greet(mirror)
-    greet(after)
-    for c in columns[1:]:
-        greet((frame, row, c))
-
-    def greet_row(number, carry):
-        greet((frame, lax.rem(row + number, 16), col))
-        return carry
-
-    lax.fori_loop(1, 16, greet_row, 0)
-    for step in range(1, 4):
-        greet((lax.rem(frame + step, 4), row, col))
     pl.semaphore_wait(barrier, 2 + 7 + 15 + 3)
 
     def send(source, target, phase, device):
@@ -373,25 +373,25 @@
     def block(number, size):
         return pl.ds(pl.multiple_of(number * size, size), size)
 
+    def send_partner(number):
+        plane, a, part = number // 8, number // 4 % 2, number % 4
+        rows = block(part, 64)
+        source = (real_ref, imaginary_ref)[plane]
+        send(source.at[2 + a, rows], partner.at[plane, a, rows], 3, mirror)
+
     each_col(
         lambda c: send(
             object_ref.at[8 * frame + c], object_rows.at[col], 0, (frame, row, c)
         )
     )
+    for number in range(6):
+        send_partner(number)
     for load in transfer_loads:
         load.wait()
     for plane in range(2):
         extra_send[plane] = transfer[plane, 0, pl.ds(0, 32, stride=8), :]
-    def send_partner(number):
-        plane, a, part = number // 8, lax.rem(number // 4, 2), lax.rem(number, 4)
-        rows = block(part, 64)
-        send(transfer.at[plane, 2 + a, rows], partner.at[plane, a, rows], 3, mirror)
-
     def send_image(c):
         send(images_ref.at[pl.ds(4 * c, 4)], image_rows.at[col], 1, (frame, row, c))
-
-    for number in range(6):
-        send_partner(number)
 
     def field_of(read):
         return jnp.concatenate(

time: 158 us -> 158 us (level)
  no operation moved by 1% of the time
where the time goes in v4:
time: 158 us
  Pallas kernels  156 us (99%)
    pallas_call x1, Pallas kernels, shards(): pl.pallas_call(kernel, out_shape=jax.ShapeDtypeStruct((8, 4, 8, 128), F32...  156 us

profile of v4, /device:TPU:1, one launch (start us, length us, event | category | flops | bytes accessed | tf_op | source)
XLA Modules:
  0.0 157.7 jit_solution(8888927340167832527)
XLA Ops:
  0.0 156.1 %gradient.1 = f32[8,4,8,128]{3,2,1,0:T(8,128)} custom-call(f32[32,4,8,128]{3,2,1,0:T(8,128)} %bitcast.20, f32[32,4,8,128]{3,2,1,0:T(8,128)} %bitcast.21, f32[4,256,128]{2,1,0:T(8,128)} %bitcast.22, f32[4,256,128]{2,1,0:T(8,128)} %bitcast.23, bf16[512,128]{1,0:T(8,128)(2,1)} %constant.28.clone.refs_4_, f32[256,256]{1,0:T(8,128)} %constant.29.clone.refs_5_, ...), custom_call_target="tpu_custom_call" | custom-call | tf_op jit(solution)/shard_map/gradient/pallas_call | solution.py:674
  156.1 1.6 copy.20
